TPU v7x, 1024 devices: a whole 4x8x16 slice. The times are simulated.
1024 devices in a mesh: dp: 16 (over y, core), expert: 4 (over x), mp: 16 (over z).
Axes of the slice: x: 4, y: 8, z: 16, core: 2. Of those that a mesh axis runs over, the one named last changes fastest.
Arguments:
- grad_out: bfloat16 [8192, 3072], P(('dp', 'expert'), 'mp'), may hold values from -6 to 6
- routing: int32 [8192, 2], P(('dp', 'expert')), may hold values from 0 to 3, all different within a row; in each aligned block of 128 rows (0 to 127, 128 to 255, ...) at most 96 rows name the same one
- gates: float32 [8192, 2], P(('dp', 'expert')), may hold values from 0.1 to 1
- hidden: bfloat16 [16, 4, 384, 8192], P('dp', 'expert', None, 'mp'), may hold values from -6 to 6
- error: bfloat16 [16, 4, 8192, 3072], P('dp', 'expert', 'mp'), may hold values from -24 to 24
- q_init: float32 [4, 4, 3072], P('expert'), may hold values from -0.109375 to 0.109375
Outputs:
- p_factor: float32 [4, 4, 8192], P('expert', None, 'mp')
- q_factor: float32 [4, 4, 3072], P('expert')
Inputs may be any that keep to these rules, and one draw needn't show every extreme that they name: `routing`: the two experts of a row differ. In the rows of one device no expert is named more than 96 times, and in some device's rows an expert is named exactly 96 times.
All inputs are finite; a program needn't handle non-finite values.
Results may differ from a plain program's by a relative error of at most 0.0032.
Values may be sent and summed in bfloat16 or wider, within the bound.
A program may use at most 32 MiB of HBM per device.

v0:
```python
import math

import jax
import jax.numpy as jnp
from jax import lax
from jax.sharding import PartitionSpec as P

FF = 8192


precise = lax.Precision.HIGHEST


def dispatch_block(token_rows, routes_block, gates_block, groups, capacity):
    flat_ids = routes_block.reshape(-1)
    onehot = (flat_ids[:, None] == jnp.arange(groups, dtype=jnp.int32)[None, :]).astype(jnp.int32)
    before = jnp.cumsum(onehot, axis=0) - onehot
    slot_index = jnp.sum(before * onehot, axis=1)
    target = flat_ids * capacity + slot_index
    placement = (target[:, None] == jnp.arange(groups * capacity, dtype=jnp.int32)[None, :]).astype(
        jnp.bfloat16
    )
    weights = gates_block.reshape(-1)[:, None]
    doubled = jnp.repeat(token_rows, routes_block.shape[1], axis=0).astype(jnp.float32)
    scaled = (weights * doubled).astype(jnp.bfloat16)
    outgoing = jnp.einsum("rs,rd->sd", placement, scaled, preferred_element_type=jnp.float32)
    return outgoing.astype(jnp.bfloat16).reshape(groups, capacity, token_rows.shape[1])


def shards(grad_out, routing, gates, hidden, error, q_init):
    groups = lax.axis_size("expert")
    slot_count = hidden.shape[2]
    capacity = slot_count // groups
    local_hidden = hidden[0, 0]
    local_error = error[0, 0]
    q_start = q_init[0]
    outgoing = dispatch_block(grad_out, routing, gates, groups, capacity)
    incoming = lax.all_to_all(outgoing, "expert", split_axis=0, concat_axis=0, tiled=True)
    slot_blocks = local_hidden.reshape(groups, capacity, local_hidden.shape[1])
    gradient = jnp.einsum(
        "scf,scd->fd",
        slot_blocks,
        lax.all_gather(incoming, "mp", axis=2, tiled=True),
        preferred_element_type=jnp.float32,
    )
    merged = gradient + local_error.astype(jnp.float32)
    p_local = jnp.einsum("kd,fd->kf", q_start, merged, precision=precise)
    p_raw = lax.psum(p_local, "dp")
    gathered = lax.all_gather(p_raw, "mp", axis=1, tiled=True)
    gram_matrix = jnp.dot(gathered, gathered.T, precision=precise)
    lower_factor = jnp.linalg.cholesky(gram_matrix)
    p_orth = lax.linalg.triangular_solve(lower_factor, p_raw, left_side=True, lower=True)
    q_local = jnp.einsum("kf,fd->kd", p_orth, merged, precision=precise)
    q_total = lax.psum(q_local, ("dp", "mp")) / lax.axis_size("dp")
    return ((p_orth * math.sqrt(FF))[None], q_total[None])


def solution(mesh):
    in_specs = (
        P(("dp", "expert"), "mp"),
        P(("dp", "expert"), None),
        P(("dp", "expert"), None),
        P("dp", "expert", None, "mp"),
        P("dp", "expert", "mp", None),
        P("expert", None, None),
    )
    out_specs = (P("expert", None, "mp"), P("expert", None, None))
    return jax.shard_map(shards, mesh=mesh, in_specs=in_specs, out_specs=out_specs, check_vma=False)
```

profile of v0, /device:TPU:1, one launch (start us, length us, event | category | flops | bytes accessed | tf_op | source)
XLA Modules:
  0.0 1156.0 jit_solution(17453653287003485988)
XLA Ops:
  7.2 0.0 copy-start
  7.2 0.0 all-gather.2.cloned.1.call-start
  7.2 0.8 copy.15
  8.1 0.1 reshape.49
  8.2 0.1 eq.39
  8.3 1.2 reduce-window.6
  9.6 0.1 slice.18
  9.6 0.1 copy.17
  9.8 0.1 copy.18
  9.9 0.1 add_bitcast_fusion
  10.0 0.8 copy.19
  10.8 0.1 mul.32
  10.9 0.9 copy.20
  11.8 0.1 broadcast_in_dim.12
  11.9 0.2 convert_element_type.30
  12.1 0.3 convolution_convert_fusion
  12.5 0.1 reshape.51
  12.7 9.9 all_to_all.5
  22.6 0.0 all-gather.2.cloned.1.call-update
  22.6 3.2 copy.22
  25.8 75.8 %all-gather.2.cloned.1.call-done = bf16[4,96,3072]{1,2,0:T(8,128)(2,1)} async-done(((bf16[4,96,192]{1,2,0:T(8,128)(2,1)}), bf16[4,96,3072]{1,2,0:T(8,128)(2,1)}) %all-gather.2.cloned.1.call-update) | async-done | bytes 2359312 | tf_op jit(solution)/shard_map/all_gather | solution.py:43
  101.6 0.0 copy-done
  101.6 0.0 copy-start.2
  101.6 3.8 convert_add_fusion
  105.4 0.0 copy-start.1
  105.4 2.7 copy-done.1
  108.1 0.0 copy-done.2
  108.1 3.4 convolution_bitcast_fusion
  111.4 33.0 %psum.14 = f32[4,512]{1,0:T(4,128)S(1)} all-reduce(f32[4,512]{1,0:T(4,128)S(1)} %convolution_bitcast_fusion), channel_id=1, replica_groups=mesh['dp'=16,'expert'=4,'mp'=16] {'dp'}, use_global_device_ids=true, to_apply=%region_3.4 | all-reduce | flops 2048 | bytes 16384 | tf_op jit(solution)/shard_map/psum | solution.py:48
  144.4 22.2 %all_gather.7 = f32[4,8192]{1,0:T(4,128)S(1)} all-gather(f32[4,512]{1,0:T(4,128)S(1)} %psum.14), channel_id=1, replica_groups=mesh['dp'=16,'expert'=4,'mp'=16] {'mp'}, dimensions={1}, use_global_device_ids=true | all-gather | bytes 139264 | tf_op jit(solution)/shard_map/all_gather | solution.py:49
  166.6 0.7 fusion.10
  167.3 0.1 copy.23
  167.4 0.4 cholesky.16
  167.8 0.6 compare_reduce_fusion
  168.5 0.6 fusion.6
  169.1 0.3 custom-call.6
  169.5 0.2 fusion.7
  169.7 7.9 fusion.11
  177.6 0.6 multiply_bitcast_fusion.1
  178.2 970.3 %psum.15 = f32[4,3072]{1,0:T(4,128)S(1)} all-reduce(f32[4,3072]{1,0:T(4,128)S(1)} %fusion.11), channel_id=1, replica_groups=mesh['dp'=16,'expert'=4,'mp'=16] {'dp','mp'}, use_global_device_ids=true, to_apply=%region_6.7 | all-reduce | flops 12288 | bytes 98304 | tf_op jit(solution)/shard_map/psum | solution.py:54
  1148.5 0.6 multiply_bitcast_fusion
  (8 shorter events, 0.2 us)
Async XLA Ops:
  7.2 94.4 %copy-start = (bf16[1,1,384,512]{3,2,1,0:T(8,128)(2,1)S(1)}, bf16[1,1,384,512]{3,2,1,0:T(8,128)(2,1)}, u32[]{:S(2)}) copy-start(bf16[1,1,384,512]{3,2,1,0:T(8,128)(2,1)} %param.9) | copy-start | bytes 1179652
  7.2 94.4 %all-gather.2.cloned.1.call-start = ((), (), s32[]{:S(2)}) async-start(), calls=%async_computation.1 | async-start | bytes 3342336 | tf_op jit(solution)/shard_map/all_gather | solution.py:43
  101.6 6.4 copy-start.2
  105.4 2.7 copy-start.1
Sparse Core Ops, SparseCore 0:
  22.7 78.8 all-gather.1
where the time goes:
time: 1170 us; the launch traced here: 1160 us
  blocking collectives  1040 us (89%)
  waiting for transfers between devices  75.8 us (6%)
  matrix products  16.3 us (1%)
  between operations  14.2 us (1%)
    psum x1, blocking collectives, shards(): q_total = lax.psum(q_local, ('dp', 'mp')) / lax.axis_size('dp')  970 us
    all_gather x1, waiting for transfers between devices, shards(): lax.all_gather(incoming, 'mp', axis=2, tiled=True)  75.8 us
    psum x1, blocking collectives, shards(): p_raw = lax.psum(p_local, 'dp')  33 us
  transfers between devices with their start and end apart: 1, of which 1 were waited for; matrix products, arithmetic and copies ran while one was open for 0% of the time, Pallas kernels for 0%

commit v1 on v0

v1 whole, which is shorter than its diff:
```python
import functools
import math

import jax
import jax.numpy as jnp
from jax import lax
from jax.experimental import pallas as pl
from jax.experimental.pallas import tpu as pltpu
from jax.sharding import PartitionSpec as P

MESH = pl.DeviceIdType.MESH
F32 = jnp.float32
BF16 = jnp.bfloat16
NT = (((1,), (1,)), ((), ()))
NN = (((1,), (0,)), ((), ()))


def split(x):
    high = x.astype(BF16)
    low = (x - high.astype(F32)).astype(BF16)
    return jnp.concatenate([high, low], axis=0)


def mul(x, y, dims):
    both = lax.dot_general(split(x), y, dims, preferred_element_type=F32)
    return both[0:4] + both[4:8]


def total(ref):
    acc = ref[0]
    for i in range(1, ref.shape[0]):
        acc = acc + ref[i]
    return acc


def bytes_of(ref, sem):
    return pltpu.make_async_copy(ref, ref, sem)


def kernel(
    sizes, ff, cap,
    gT_hbm, rT_hbm, gateT_hbm, h_hbm, e_hbm, q_hbm,
    p_out, q_out,
    gT, rT, gateT, h, e, q,
    outT, incT, ipk, qe, zb, pb, xb, gb, pes, peb, vb, fb,
    load_sem, a_send, a_recv, b_send, b_recv, c_send, c_recv, d_send, d_recv, g_send, g_recv, w_send, w_recv,
    v_send, v_recv, f_send, f_recv, far_sem,
):
    n_dp, n_ex, n_mp = sizes
    d, s, m = lax.axis_index("dp"), lax.axis_index("expert"), lax.axis_index("mp")
    slots = h.shape[0]
    far = n_mp // 4

    def peer(axis, me, n, i):
        return {axis: lax.rem(me + i, n)}

    small = [(gT_hbm, gT), (rT_hbm, rT), (gateT_hbm, gateT), (q_hbm.at[0], q), (h_hbm.at[0, 0], h)]
    loads = [pltpu.make_async_copy(a, b, load_sem.at[i]) for i, (a, b) in enumerate(small)]
    rows = e.shape[0] // 4
    for i in range(4):
        part = pl.ds(i * rows, rows)
        loads.append(pltpu.make_async_copy(e_hbm.at[0, 0, part], e.at[part], load_sem.at[len(small) + i]))

    barrier = pltpu.get_barrier_semaphore()
    near = [i for i in range(1, n_mp) if min(i, n_mp - i) <= far]
    for i in near:
        pl.semaphore_signal(barrier, inc=1, device_id=peer("mp", m, n_mp, i), device_id_type=MESH)
    for i in range(1, n_dp):
        pl.semaphore_signal(barrier, inc=1, device_id=peer("dp", d, n_dp, i), device_id_type=MESH)
    for i in range(1, n_ex):
        pl.semaphore_signal(barrier, inc=1, device_id=peer("expert", s, n_ex, i), device_id_type=MESH)
    for copy in loads:
        copy.start()

    for i in range(3):
        loads[i].wait()
    tokens = gT.shape[1]
    feats = gT.shape[0]
    r0, r1 = rT[0:1, :], rT[1:2, :]
    g0, g1 = gateT[0:1, :], gateT[1:2, :]
    ids = lax.broadcasted_iota(jnp.int32, (8, tokens), 0)
    hits = jnp.where((ids == r0) | (ids == r1), 1.0, 0.0).astype(F32)
    row = lax.broadcasted_iota(jnp.int32, (tokens, tokens), 0)
    col = lax.broadcasted_iota(jnp.int32, (tokens, tokens), 1)
    earlier = jnp.where(row < col, 1.0, 0.0).astype(BF16)
    before = lax.dot_general(hits.astype(BF16), earlier, NN, preferred_element_type=F32)
    place = jnp.where(hits > 0.5, before, -1.0).astype(jnp.int32)
    grads = gT[...].astype(F32)
    for i in range(n_ex):
        gate = jnp.where(r0 == i, g0, 0.0) + jnp.where(r1 == i, g1, 0.0)
        scaled = (grads * gate).astype(BF16)
        placement = jnp.where(row == place[i : i + 1, :], 1.0, 0.0).astype(BF16)
        outT[i] = lax.dot_general(scaled, placement, NT, preferred_element_type=F32).astype(BF16)
    odd = lax.rem(m, 2)
    window = pl.ds(pl.multiple_of(64 * odd, 64), feats)
    edge = pl.ds(pl.multiple_of(feats * (1 - odd), 64), 64)
    for i in range(n_ex):
        incT[i, edge, :] = jnp.zeros((64, tokens), BF16)
    incT[s, window, :] = outT[s]
    gb[m] = jnp.zeros(gb.shape[1:], F32)

    pl.semaphore_wait(barrier, len(near) + n_dp - 1 + n_ex - 1)
    sends = []
    for i in range(1, n_ex):
        there = lax.rem(s + i, n_ex)
        pltpu.make_async_remote_copy(
            src_ref=outT.at[there], dst_ref=incT.at[s, window], send_sem=a_send, recv_sem=a_recv,
            device_id={"expert": there}, device_id_type=MESH,
        ).start()
    for i in (far, n_mp - far):
        pl.semaphore_signal(far_sem, inc=1, device_id=peer("mp", m, n_mp, i), device_id_type=MESH)

    loads[3].wait()
    start = pl.multiple_of(feats * m - 64 * odd, 128)
    q_win = q[:, pl.ds(start, 256)]
    lane = lax.broadcasted_iota(jnp.int32, (4, 256), 1)
    q_win = jnp.where((lane >= 64 * odd) & (lane < 64 * odd + feats), q_win, 0.0)
    q_two = split(q_win)

    def exchange(axis, me, n, buf, send_sem, recv_sem, src=None):
        for i in range(1, n):
            there = lax.rem(me + i, n)
            pltpu.make_async_remote_copy(
                src_ref=buf.at[me] if src is None else src.at[there], dst_ref=buf.at[me],
                send_sem=send_sem, recv_sem=recv_sem, device_id={axis: there}, device_id_type=MESH,
            ).start()

    bytes_of(outT.at[pl.ds(0, n_ex - 1)], a_recv).wait()
    z_parts = []
    for i in range(n_ex):
        both = lax.dot_general(q_two, incT[i], NN, preferred_element_type=F32)
        z_parts.append((both[0:4] + both[4:8])[:, 0:cap])
    zb[m] = jnp.concatenate(z_parts, axis=1)
    pl.semaphore_wait(far_sem, 2)
    exchange("mp", m, n_mp, zb, b_send, b_recv)

    q_all = split(q[...])
    for i in range(4):
        loads[5 + i].wait()
        both = lax.dot_general(q_all, e[i * rows : (i + 1) * rows, :], NT, preferred_element_type=F32)
        qe[:, i * rows : (i + 1) * rows] = both[0:4] + both[4:8]
    ipk[...] = jnp.concatenate([incT[i].astype(F32)[:, 0:cap] for i in range(n_ex)], axis=1).astype(BF16)
    loads[4].wait()

    bytes_of(zb.at[pl.ds(0, n_mp - 1)], b_recv).wait()
    pb[d] = mul(total(zb), h[...], NN) + qe[...]
    exchange("dp", d, n_dp, pb, c_send, c_recv)
    bytes_of(pb.at[pl.ds(0, n_dp - 1)], c_recv).wait()
    p_raw = total(pb)

    xb[m] = mul(p_raw, h[...], NT)
    exchange("mp", m, n_mp, xb, d_send, d_recv)

    both = lax.dot_general(split(p_raw), e[...], NN, preferred_element_type=F32)
    pe = both[0:4] + both[4:8]
    for i in range(n_mp):
        skip = 64 * (i % 2)
        part = pe[:, feats * i - skip : feats * i - skip + 256] if feats * i - skip + 256 <= pe.shape[1] else None
        pes[i] = jnp.where((lane >= skip) & (lane < skip + feats), part, 0.0)
    peb[m] = pes[m]
    exchange("mp", m, n_mp, peb, w_send, w_recv, src=pes)
    gram = lax.dot_general(p_raw, p_raw, NT, precision=lax.Precision.HIGHEST, preferred_element_type=F32)
    gb[m, :, 0:4] = gram
    exchange("mp", m, n_mp, gb, g_send, g_recv)

    bytes_of(xb.at[pl.ds(0, n_mp - 1)], d_recv).wait()
    right = mul(total(xb), ipk[...], NT)
    bytes_of(peb.at[pl.ds(0, n_mp - 1)], w_recv).wait()
    vb[d] = right + total(peb)
    exchange("dp", d, n_dp, vb, v_send, v_recv)

    bytes_of(gb.at[pl.ds(0, n_mp - 1)], g_recv).wait()
    g = total(gb)
    low = [[None] * 4 for _ in range(4)]
    inv = [None] * 4
    for i in range(4):
        for j in range(i + 1):
            acc = g[i : i + 1, j : j + 1]
            for k in range(j):
                acc = acc - low[i][k] * low[j][k]
            if i == j:
                root = jnp.sqrt(acc)
                inv[i] = 1.0 / root
            else:
                low[i][j] = acc * inv[j]

    def solve(x, scale):
        done = []
        for i in range(4):
            acc = x[i : i + 1, :]
            for k in range(i):
                acc = acc - low[i][k] * done[k]
            done.append(acc * inv[i])
        return jnp.concatenate(done, axis=0) * scale

    p_out[0] = solve(p_raw, math.sqrt(ff))

    bytes_of(vb.at[pl.ds(0, n_dp - 1)], v_recv).wait()
    fb[m] = solve(total(vb), 1.0 / n_dp)
    exchange("mp", m, n_mp, fb, f_send, f_recv)
    bytes_of(fb.at[pl.ds(0, n_mp - 1)], f_recv).wait()
    for i in range(0, n_mp, 2):
        even, uneven = fb[i], fb[i + 1]
        q_out[0, :, feats * i : feats * i + 128] = even[:, 0:128]
        q_out[0, :, feats * i + 128 : feats * i + 256] = even[:, 128:256] + uneven[:, 0:128]
        q_out[0, :, feats * i + 256 : feats * i + 384] = uneven[:, 128:256]

    bytes_of(outT.at[pl.ds(0, n_ex - 1)], a_send).wait()
    for buf, sem, n in ((zb, b_send, n_mp), (pb, c_send, n_dp), (xb, d_send, n_mp), (gb, g_send, n_mp),
                        (peb, w_send, n_mp), (vb, v_send, n_dp), (fb, f_send, n_mp)):
        bytes_of(buf.at[pl.ds(0, n - 1)], sem).wait()


def shards(grad_out, routing, gates, hidden, error, q_init):
    sizes = (lax.axis_size("dp"), lax.axis_size("expert"), lax.axis_size("mp"))
    n_dp, n_ex, n_mp = sizes
    tokens, feats = grad_out.shape
    slots, units = hidden.shape[2:]
    width = error.shape[3]
    rank = q_init.shape[1]
    dma = pltpu.SemaphoreType.DMA
    return pl.pallas_call(
        functools.partial(kernel, sizes, units * n_mp, slots // n_ex),
        out_shape=(
            jax.ShapeDtypeStruct((1, rank, units), F32),
            jax.ShapeDtypeStruct((1, rank, width), F32),
        ),
        in_specs=[pl.BlockSpec(memory_space=pltpu.HBM)] * 6,
        out_specs=(pl.BlockSpec(memory_space=pltpu.VMEM), pl.BlockSpec(memory_space=pltpu.VMEM)),
        scratch_shapes=[
            pltpu.VMEM((feats, tokens), BF16),
            pltpu.VMEM((2, tokens), jnp.int32),
            pltpu.VMEM((2, tokens), F32),
            pltpu.VMEM((slots, units), BF16),
            pltpu.VMEM((units, width), BF16),
            pltpu.VMEM((rank, width), F32),
            pltpu.VMEM((n_ex, feats, tokens), BF16),
            pltpu.VMEM((n_ex, 256, tokens), BF16),
            pltpu.VMEM((256, slots), BF16),
            pltpu.VMEM((rank, units), F32),
            pltpu.VMEM((n_mp, rank, slots), F32),
            pltpu.VMEM((n_dp, rank, units), F32),
            pltpu.VMEM((n_mp, rank, slots), F32),
            pltpu.VMEM((n_mp, rank, 128), F32),
            pltpu.VMEM((n_mp, rank, 256), F32),
            pltpu.VMEM((n_mp, rank, 256), F32),
            pltpu.VMEM((n_dp, rank, 256), F32),
            pltpu.VMEM((n_mp, rank, 256), F32),
            dma((9,)),
        ] + [dma(())] * 16 + [pltpu.SemaphoreType.REGULAR],
        compiler_params=pltpu.CompilerParams(
            collective_id=0, has_side_effects=True, vmem_limit_bytes=60 * 1024 * 1024
        ),
        name="compress",
    )(grad_out.T, routing.T, gates.T, hidden, error, q_init)


def solution(mesh):
    in_specs = (
        P(("dp", "expert"), "mp"),
        P(("dp", "expert"), None),
        P(("dp", "expert"), None),
        P("dp", "expert", None, "mp"),
        P("dp", "expert", "mp", None),
        P("expert", None, None),
    )
    out_specs = (P("expert", None, "mp"), P("expert", None, None))
    return jax.shard_map(shards, mesh=mesh, in_specs=in_specs, out_specs=out_specs, check_vma=False)
```

time: 1170 us -> 74.5 us (0.06); the launches traced: 1160 us -> 74.3 us
  blocking collectives: 1040 us -> 0 us
  waiting for transfers between devices: 75.8 us -> 0 us
  Pallas kernels: 0 us -> 70.9 us
  matrix products: 16.3 us -> 0 us
  between operations: 14.2 us -> 0.64 us
    psum x2 -> x0, blocking collectives: 1000 us -> none  [the longest x1 970 us: shards(): q_total = lax.psum(q_local, ('dp', 'mp')) / lax.axis_size('dp')]
    all_gather x1 -> x0, waiting for transfers between devices: 75.8 us -> none  [shards(): lax.all_gather(incoming, 'mp', axis=2, tiled=True)]
    pallas_call x0 -> x1, Pallas kernels: none -> 70.9 us  [shards(): pl.pallas_call(functools.partial(kernel, sizes, units * n_mp, slots // n_...]
    all_gather x1 -> x0, blocking collectives: 22.2 us -> none  [shards(): gathered = lax.all_gather(p_raw, 'mp', axis=1, tiled=True)]
    dot_general x5 -> x0, matrix products: 16.1 us -> none  [the longest x1 7.93 us: shards(): q_local = jnp.einsum('kf,fd->kd', p_orth, merged, precision=precise)]
  transfers between devices with their start and end apart: 1 -> 0, of which waited for: 1 -> 0; matrix products, arithmetic and copies ran while one was open for 0% -> 0% of each run, Pallas kernels for 0% -> 0%
where the time goes in v1:
time: 74.5 us; the launch traced here: 74.3 us
  Pallas kernels  70.9 us (95%)
  local copies, waits for them, and re-layouts  2.72 us (4%)
    pallas_call x1, Pallas kernels, shards(): pl.pallas_call(functools.partial(kernel, sizes, units * n_mp, slots // n_...  70.9 us
    unnamed x2, local copies, waits for them, and re-layouts  2.72 us

profile of v1, /device:TPU:1, one launch (start us, length us, event | category | flops | bytes accessed | tf_op | source)
XLA Modules:
  0.0 74.3 jit_solution(12325586012442966841)
XLA Ops:
  0.6 70.9 %compress.1 = (f32[1,4,512]{2,1,0:T(4,128)}, f32[1,4,3072]{2,1,0:T(4,128)}) custom-call(bf16[192,128]{1,0:T(8,128)(2,1)} %bitcast.3, s32[2,128]{1,0:T(2,128)} %bitcast.4, f32[2,128]{1,0:T(2,128)} %bitcast.5, bf16[1,1,384,512]{3,2,1,0:T(8,128)(2,1)} %h_hbm.1, bf16[1,1,512,3072]{3,2,1,0:T(8,128)(2,1)} %e_hbm.1, f32[1,4,3072]{2,1,0:T(4,128)} %q_hbm.1), custom_call_target="tpu_custom_call" | custom-call | tf_op jit(solution)/shard_map/compress/pallas_call | solution.py:222
  71.6 1.3 %copy.10 = f32[1,4,512]{2,1,0:T(4,128)} copy(f32[1,4,512]{2,1,0:T(4,128)} %get-tuple-element.4) | data formatting | bytes 16384
  72.9 1.4 %copy.11 = f32[1,4,3072]{2,1,0:T(4,128)} copy(f32[1,4,3072]{2,1,0:T(4,128)} %get-tuple-element.5) | data formatting | bytes 98304

commit v2 on v1

--- a/solution.py
+++ b/solution.py
@@ -42,14 +42,17 @@
     gT_hbm, rT_hbm, gateT_hbm, h_hbm, e_hbm, q_hbm,
     p_out, q_out,
     gT, rT, gateT, h, e, q,
-    outT, incT, ipk, qe, zb, pb, xb, gb, pes, peb, vb, fb,
-    load_sem, a_send, a_recv, b_send, b_recv, c_send, c_recv, d_send, d_recv, g_send, g_recv, w_send, w_recv,
-    v_send, v_recv, f_send, f_recv, far_sem,
+    outT, incT, ipk, qe, zb, pb, xb, pes, yb, ab, vb, fb, lb,
+    load_sem, a_send, a_recv, b_send, b_recv, c_send, c_recv, d_send, d_recv, g_send, g_recv, y_send, y_recv,
+    v_send, v_recv, f_send, f_recv, l_send, l_recv, far_sem,
 ):
     n_dp, n_ex, n_mp = sizes
     d, s, m = lax.axis_index("dp"), lax.axis_index("expert"), lax.axis_index("mp")
     slots = h.shape[0]
     far = n_mp // 4
+    around = sorted(range(1, n_mp), key=lambda i: -min(i, n_mp - i))
+    along = sorted(range(1, n_dp), key=lambda i: -min(i // 2, n_dp // 2 - i // 2))
+    offsets = {"mp": around, "dp": along}
 
     def peer(axis, me, n, i):
         return {axis: lax.rem(me + i, n)}
@@ -62,14 +65,16 @@
         loads.append(pltpu.make_async_copy(e_hbm.at[0, 0, part], e.at[part], load_sem.at[len(small) + i]))
 
     barrier = pltpu.get_barrier_semaphore()
-    near = [i for i in range(1, n_mp) if min(i, n_mp - i) <= far]
+    near = [i for i in around if min(i, n_mp - i) <= far]
+    for copy in loads[0:3]:
+        copy.start()
+    for i in range(1, n_ex):
+        pl.semaphore_signal(barrier, inc=1, device_id=peer("expert", s, n_ex, i), device_id_type=MESH)
     for i in near:
         pl.semaphore_signal(barrier, inc=1, device_id=peer("mp", m, n_mp, i), device_id_type=MESH)
-    for i in range(1, n_dp):
+    for i in along:
         pl.semaphore_signal(barrier, inc=1, device_id=peer("dp", d, n_dp, i), device_id_type=MESH)
-    for i in range(1, n_ex):
-        pl.semaphore_signal(barrier, inc=1, device_id=peer("expert", s, n_ex, i), device_id_type=MESH)
-    for copy in loads:
+    for copy in loads[3:]:
         copy.start()
 
     for i in range(3):
@@ -97,11 +102,9 @@
     for i in range(n_ex):
         incT[i, edge, :] = jnp.zeros((64, tokens), BF16)
     incT[s, window, :] = outT[s]
-    gb[m] = jnp.zeros(gb.shape[1:], F32)
 
     pl.semaphore_wait(barrier, len(near) + n_dp - 1 + n_ex - 1)
-    sends = []
-    for i in range(1, n_ex):
+    for i in sorted(range(1, n_ex), key=lambda i: -min(i, n_ex - i)):
         there = lax.rem(s + i, n_ex)
         pltpu.make_async_remote_copy(
             src_ref=outT.at[there], dst_ref=incT.at[s, window], send_sem=a_send, recv_sem=a_recv,
@@ -118,7 +121,7 @@
     q_two = split(q_win)
 
     def exchange(axis, me, n, buf, send_sem, recv_sem, src=None):
-        for i in range(1, n):
+        for i in offsets[axis]:
             there = lax.rem(me + i, n)
             pltpu.make_async_remote_copy(
                 src_ref=buf.at[me] if src is None else src.at[there], dst_ref=buf.at[me],
@@ -153,34 +156,49 @@
 
     both = lax.dot_general(split(p_raw), e[...], NN, preferred_element_type=F32)
     pe = both[0:4] + both[4:8]
-    for i in range(n_mp):
+    for i in range(n_dp):
         skip = 64 * (i % 2)
-        part = pe[:, feats * i - skip : feats * i - skip + 256] if feats * i - skip + 256 <= pe.shape[1] else None
+        part = pe[:, feats * i - skip : feats * i - skip + 256]
         pes[i] = jnp.where((lane >= skip) & (lane < skip + feats), part, 0.0)
-    peb[m] = pes[m]
-    exchange("mp", m, n_mp, peb, w_send, w_recv, src=pes)
-    gram = lax.dot_general(p_raw, p_raw, NT, precision=lax.Precision.HIGHEST, preferred_element_type=F32)
-    gb[m, :, 0:4] = gram
-    exchange("mp", m, n_mp, gb, g_send, g_recv)
+    yb[d] = pes[d]
+    exchange("dp", d, n_dp, yb, y_send, y_recv, src=pes)
+
+    tiled = jnp.concatenate([p_raw] * 4, axis=0)
+    gram = lax.dot_general(p_raw, tiled, NT, precision=lax.Precision.HIGHEST, preferred_element_type=F32)
+    own = lax.broadcasted_iota(jnp.int32, (4, 16), 0) == lax.broadcasted_iota(jnp.int32, (4, 16), 1) // 4
+    gram = jnp.sum(jnp.where(own, gram, 0.0), axis=0, keepdims=True)
+    odd_d = lax.rem(d, 2)
+    gap = jnp.zeros((1, 176), F32)
+    spare = jnp.concatenate([gap, jnp.zeros((1, 16), F32), gram, jnp.zeros((1, 48), F32)], axis=1)
+    spare = jnp.where(odd_d == 1, jnp.concatenate([gram, gap, jnp.zeros((1, 64), F32)], axis=1), spare)
+    top = lax.broadcasted_iota(jnp.int32, (4, 256), 0) == 0
+
+    bytes_of(yb.at[pl.ds(0, n_dp - 1)], y_recv).wait()
+    ab[m] = total(yb) + jnp.where(top, spare, 0.0)
+    exchange("mp", m, n_mp, ab, g_send, g_recv)
 
     bytes_of(xb.at[pl.ds(0, n_mp - 1)], d_recv).wait()
-    right = mul(total(xb), ipk[...], NT)
-    bytes_of(peb.at[pl.ds(0, n_mp - 1)], w_recv).wait()
-    vb[d] = right + total(peb)
+    vb[d] = mul(total(xb), ipk[...], NT)
     exchange("dp", d, n_dp, vb, v_send, v_recv)
-
-    bytes_of(gb.at[pl.ds(0, n_mp - 1)], g_recv).wait()
-    g = total(gb)
+    bytes_of(vb.at[pl.ds(0, n_dp - 1)], v_recv).wait()
+    fb[m] = total(vb)
+    exchange("mp", m, n_mp, fb, f_send, f_recv)
+
+    bytes_of(ab.at[pl.ds(0, n_mp - 1)], g_recv).wait()
+    mixed = total(ab)
+    lb[d] = jnp.where((lane >= 64 * odd_d) & (lane < 64 * odd_d + feats), mixed, 0.0)
+    exchange("dp", d, n_dp, lb, l_send, l_recv)
+
+    g = jnp.where(odd_d == 1, mixed[0:1, 0:16], mixed[0:1, 192:208])
     low = [[None] * 4 for _ in range(4)]
     inv = [None] * 4
     for i in range(4):
         for j in range(i + 1):
-            acc = g[i : i + 1, j : j + 1]
+            acc = g[:, 4 * i + j : 4 * i + j + 1]
             for k in range(j):
                 acc = acc - low[i][k] * low[j][k]
             if i == j:
-                root = jnp.sqrt(acc)
-                inv[i] = 1.0 / root
+                inv[i] = 1.0 / jnp.sqrt(acc)
             else:
                 low[i][j] = acc * inv[j]
 
@@ -195,19 +213,16 @@
 
     p_out[0] = solve(p_raw, math.sqrt(ff))
 
-    bytes_of(vb.at[pl.ds(0, n_dp - 1)], v_recv).wait()
-    fb[m] = solve(total(vb), 1.0 / n_dp)
-    exchange("mp", m, n_mp, fb, f_send, f_recv)
+    bytes_of(lb.at[pl.ds(0, n_dp - 1)], l_recv).wait()
     bytes_of(fb.at[pl.ds(0, n_mp - 1)], f_recv).wait()
     for i in range(0, n_mp, 2):
-        even, uneven = fb[i], fb[i + 1]
-        q_out[0, :, feats * i : feats * i + 128] = even[:, 0:128]
-        q_out[0, :, feats * i + 128 : feats * i + 256] = even[:, 128:256] + uneven[:, 0:128]
-        q_out[0, :, feats * i + 256 : feats * i + 384] = uneven[:, 128:256]
+        even, uneven = fb[i] + lb[i], fb[i + 1] + lb[i + 1]
+        three = jnp.concatenate([even[:, 0:128], even[:, 128:256] + uneven[:, 0:128], uneven[:, 128:256]], axis=1)
+        q_out[0, :, feats * i : feats * i + 384] = solve(three, 1.0 / n_dp)
 
     bytes_of(outT.at[pl.ds(0, n_ex - 1)], a_send).wait()
-    for buf, sem, n in ((zb, b_send, n_mp), (pb, c_send, n_dp), (xb, d_send, n_mp), (gb, g_send, n_mp),
-                        (peb, w_send, n_mp), (vb, v_send, n_dp), (fb, f_send, n_mp)):
+    for buf, sem, n in ((zb, b_send, n_mp), (pb, c_send, n_dp), (xb, d_send, n_mp), (yb, y_send, n_dp),
+                        (ab, g_send, n_mp), (vb, v_send, n_dp), (fb, f_send, n_mp), (lb, l_send, n_dp)):
         bytes_of(buf.at[pl.ds(0, n - 1)], sem).wait()
 
 
@@ -222,8 +237,8 @@
     return pl.pallas_call(
         functools.partial(kernel, sizes, units * n_mp, slots // n_ex),
         out_shape=(
-            jax.ShapeDtypeStruct((1, rank, units), F32),
-            jax.ShapeDtypeStruct((1, rank, width), F32),
+            pltpu.VMEM((1, rank, units), F32),
+            pltpu.VMEM((1, rank, width), F32),
         ),
         in_specs=[pl.BlockSpec(memory_space=pltpu.HBM)] * 6,
         out_specs=(pl.BlockSpec(memory_space=pltpu.VMEM), pl.BlockSpec(memory_space=pltpu.VMEM)),
@@ -241,13 +256,14 @@
             pltpu.VMEM((n_mp, rank, slots), F32),
             pltpu.VMEM((n_dp, rank, units), F32),
             pltpu.VMEM((n_mp, rank, slots), F32),
-            pltpu.VMEM((n_mp, rank, 128), F32),
+            pltpu.VMEM((n_dp, rank, 256), F32),
+            pltpu.VMEM((n_dp, rank, 256), F32),
             pltpu.VMEM((n_mp, rank, 256), F32),
+            pltpu.VMEM((n_dp, rank, 256), F32),
             pltpu.VMEM((n_mp, rank, 256), F32),
             pltpu.VMEM((n_dp, rank, 256), F32),
-            pltpu.VMEM((n_mp, rank, 256), F32),
             dma((9,)),
-        ] + [dma(())] * 16 + [pltpu.SemaphoreType.REGULAR],
+        ] + [dma(())] * 18 + [pltpu.SemaphoreType.REGULAR],
         compiler_params=pltpu.CompilerParams(
             collective_id=0, has_side_effects=True, vmem_limit_bytes=60 * 1024 * 1024
         ),

time: 74.5 us -> 62.3 us (0.84)
  Pallas kernels: 70.9 us -> 60.3 us
  local copies, waits for them, and re-layouts: 2.72 us -> 1.22 us
    pallas_call x1, Pallas kernels: 70.9 us -> 60.3 us  [shards(): pl.pallas_call(functools.partial(kernel, sizes, units * n_mp, slots // n_...]
    unnamed x2, local copies, waits for them, and re-layouts: 2.72 us -> 1.22 us
where the time goes in v2:
time: 62.3 us; the launch traced here: 62.1 us
  Pallas kernels  60.3 us (97%)
  local copies, waits for them, and re-layouts  1.22 us (2%)
  between operations  0.64 us (1%)
    pallas_call x1, Pallas kernels, shards(): pl.pallas_call(functools.partial(kernel, sizes, units * n_mp, slots // n_...  60.3 us

profile of v2, /device:TPU:1, one launch (start us, length us, event | category | flops | bytes accessed | tf_op | source)
XLA Modules:
  0.0 62.1 jit_solution(17689831422796258616)
XLA Ops:
  0.6 60.3 %compress.1 = (f32[1,4,512]{2,1,0:T(4,128)S(1)}, f32[1,4,3072]{2,1,0:T(4,128)S(1)}) custom-call(bf16[192,128]{1,0:T(8,128)(2,1)} %bitcast.3, s32[2,128]{1,0:T(2,128)} %bitcast.4, f32[2,128]{1,0:T(2,128)} %bitcast.5, bf16[1,1,384,512]{3,2,1,0:T(8,128)(2,1)} %h_hbm.1, bf16[1,1,512,3072]{3,2,1,0:T(8,128)(2,1)} %e_hbm.1, f32[1,4,3072]{2,1,0:T(4,128)} %q_hbm.1), custom_call_target="tpu_custom_call" | custom-call | tf_op jit(solution)/shard_map/compress/pallas_call | solution.py:237
  60.9 0.6 copy.10
  61.5 0.6 copy.11

commit v3 on v2

--- a/solution.py
+++ b/solution.py
@@ -27,10 +27,20 @@
 
 
 def total(ref):
-    acc = ref[0]
+    acc = ref[0].astype(F32)
     for i in range(1, ref.shape[0]):
-        acc = acc + ref[i]
+        acc = acc + ref[i].astype(F32)
     return acc
+
+
+def pack(x):
+    parts = [x[:, i : i + 128] for i in range(0, x.shape[1], 128)]
+    fill = 16 - 4 * len(parts)
+    return jnp.concatenate(parts + [jnp.zeros((fill, 128), F32)], axis=0).astype(BF16)
+
+
+def unpack(x, n):
+    return jnp.concatenate([x[4 * i : 4 * i + 4] for i in range(n // 128)], axis=1)
 
 
 def bytes_of(ref, sem):
@@ -41,7 +51,7 @@
     sizes, ff, cap,
     gT_hbm, rT_hbm, gateT_hbm, h_hbm, e_hbm, q_hbm,
     p_out, q_out,
-    gT, rT, gateT, h, e, q,
+    gT, rT, gateT, h, hT, e, q,
     outT, incT, ipk, qe, zb, pb, xb, pes, yb, ab, vb, fb, lb,
     load_sem, a_send, a_recv, b_send, b_recv, c_send, c_recv, d_send, d_recv, g_send, g_recv, y_send, y_recv,
     v_send, v_recv, f_send, f_recv, l_send, l_recv, far_sem,
@@ -133,7 +143,7 @@
     for i in range(n_ex):
         both = lax.dot_general(q_two, incT[i], NN, preferred_element_type=F32)
         z_parts.append((both[0:4] + both[4:8])[:, 0:cap])
-    zb[m] = jnp.concatenate(z_parts, axis=1)
+    zb[m] = pack(jnp.concatenate(z_parts, axis=1))
     pl.semaphore_wait(far_sem, 2)
     exchange("mp", m, n_mp, zb, b_send, b_recv)
 
@@ -142,24 +152,27 @@
         loads[5 + i].wait()
         both = lax.dot_general(q_all, e[i * rows : (i + 1) * rows, :], NT, preferred_element_type=F32)
         qe[:, i * rows : (i + 1) * rows] = both[0:4] + both[4:8]
-    ipk[...] = jnp.concatenate([incT[i].astype(F32)[:, 0:cap] for i in range(n_ex)], axis=1).astype(BF16)
+    for i in range(n_ex):
+        ipk[i * cap : (i + 1) * cap, :] = incT[i].T[0:cap, :]
     loads[4].wait()
+    hT[...] = h[...].T
 
     bytes_of(zb.at[pl.ds(0, n_mp - 1)], b_recv).wait()
-    pb[d] = mul(total(zb), h[...], NN) + qe[...]
+    pb[d] = mul(unpack(total(zb), slots), h[...], NN) + qe[...]
     exchange("dp", d, n_dp, pb, c_send, c_recv)
     bytes_of(pb.at[pl.ds(0, n_dp - 1)], c_recv).wait()
     p_raw = total(pb)
 
-    xb[m] = mul(p_raw, h[...], NT)
+    xb[m] = pack(mul(p_raw, hT[...], NN))
     exchange("mp", m, n_mp, xb, d_send, d_recv)
 
     both = lax.dot_general(split(p_raw), e[...], NN, preferred_element_type=F32)
     pe = both[0:4] + both[4:8]
+    quarters = n_dp // 4
+    width = pe.shape[1] // quarters
     for i in range(n_dp):
-        skip = 64 * (i % 2)
-        part = pe[:, feats * i - skip : feats * i - skip + 256]
-        pes[i] = jnp.where((lane >= skip) & (lane < skip + feats), part, 0.0)
+        k, c = i // quarters, i % quarters
+        pes[i] = pe[k : k + 1, c * width : (c + 1) * width]
     yb[d] = pes[d]
     exchange("dp", d, n_dp, yb, y_send, y_recv, src=pes)
 
@@ -167,18 +180,14 @@
     gram = lax.dot_general(p_raw, tiled, NT, precision=lax.Precision.HIGHEST, preferred_element_type=F32)
     own = lax.broadcasted_iota(jnp.int32, (4, 16), 0) == lax.broadcasted_iota(jnp.int32, (4, 16), 1) // 4
     gram = jnp.sum(jnp.where(own, gram, 0.0), axis=0, keepdims=True)
-    odd_d = lax.rem(d, 2)
-    gap = jnp.zeros((1, 176), F32)
-    spare = jnp.concatenate([gap, jnp.zeros((1, 16), F32), gram, jnp.zeros((1, 48), F32)], axis=1)
-    spare = jnp.where(odd_d == 1, jnp.concatenate([gram, gap, jnp.zeros((1, 64), F32)], axis=1), spare)
-    top = lax.broadcasted_iota(jnp.int32, (4, 256), 0) == 0
+    gram = jnp.concatenate([gram, jnp.zeros((1, 112), F32)], axis=1)
 
     bytes_of(yb.at[pl.ds(0, n_dp - 1)], y_recv).wait()
-    ab[m] = total(yb) + jnp.where(top, spare, 0.0)
+    ab[m] = jnp.concatenate([total(yb), gram], axis=1)
     exchange("mp", m, n_mp, ab, g_send, g_recv)
 
     bytes_of(xb.at[pl.ds(0, n_mp - 1)], d_recv).wait()
-    vb[d] = mul(total(xb), ipk[...], NT)
+    vb[d] = mul(unpack(total(xb), slots), ipk[...], NN)
     exchange("dp", d, n_dp, vb, v_send, v_recv)
     bytes_of(vb.at[pl.ds(0, n_dp - 1)], v_recv).wait()
     fb[m] = total(vb)
@@ -186,10 +195,10 @@
 
     bytes_of(ab.at[pl.ds(0, n_mp - 1)], g_recv).wait()
     mixed = total(ab)
-    lb[d] = jnp.where((lane >= 64 * odd_d) & (lane < 64 * odd_d + feats), mixed, 0.0)
+    lb[d] = mixed[:, 0:width]
     exchange("dp", d, n_dp, lb, l_send, l_recv)
 
-    g = jnp.where(odd_d == 1, mixed[0:1, 0:16], mixed[0:1, 192:208])
+    g = mixed[:, width : width + 16]
     low = [[None] * 4 for _ in range(4)]
     inv = [None] * 4
     for i in range(4):
@@ -205,20 +214,22 @@
     def solve(x, scale):
         done = []
         for i in range(4):
-            acc = x[i : i + 1, :]
+            acc = x[i]
             for k in range(i):
                 acc = acc - low[i][k] * done[k]
             done.append(acc * inv[i])
         return jnp.concatenate(done, axis=0) * scale
 
-    p_out[0] = solve(p_raw, math.sqrt(ff))
+    p_out[0] = solve([p_raw[i : i + 1, :] for i in range(4)], math.sqrt(ff))
 
     bytes_of(lb.at[pl.ds(0, n_dp - 1)], l_recv).wait()
     bytes_of(fb.at[pl.ds(0, n_mp - 1)], f_recv).wait()
     for i in range(0, n_mp, 2):
-        even, uneven = fb[i] + lb[i], fb[i + 1] + lb[i + 1]
+        even, uneven = fb[i], fb[i + 1]
         three = jnp.concatenate([even[:, 0:128], even[:, 128:256] + uneven[:, 0:128], uneven[:, 128:256]], axis=1)
-        q_out[0, :, feats * i : feats * i + 384] = solve(three, 1.0 / n_dp)
+        c, at = divmod(feats * i, width)
+        x = [three[k : k + 1, :] + lb[k * quarters + c][:, at : at + 384] for k in range(4)]
+        q_out[0, :, feats * i : feats * i + 384] = solve(x, 1.0 / n_dp)
 
     bytes_of(outT.at[pl.ds(0, n_ex - 1)], a_send).wait()
     for buf, sem, n in ((zb, b_send, n_mp), (pb, c_send, n_dp), (xb, d_send, n_mp), (yb, y_send, n_dp),
@@ -233,6 +244,7 @@
     slots, units = hidden.shape[2:]
     width = error.shape[3]
     rank = q_init.shape[1]
+    piece = rank * width // n_dp
     dma = pltpu.SemaphoreType.DMA
     return pl.pallas_call(
         functools.partial(kernel, sizes, units * n_mp, slots // n_ex),
@@ -247,21 +259,22 @@
             pltpu.VMEM((2, tokens), jnp.int32),
             pltpu.VMEM((2, tokens), F32),
             pltpu.VMEM((slots, units), BF16),
+            pltpu.VMEM((units, slots), BF16),
             pltpu.VMEM((units, width), BF16),
             pltpu.VMEM((rank, width), F32),
             pltpu.VMEM((n_ex, feats, tokens), BF16),
             pltpu.VMEM((n_ex, 256, tokens), BF16),
-            pltpu.VMEM((256, slots), BF16),
+            pltpu.VMEM((slots, 256), BF16),
             pltpu.VMEM((rank, units), F32),
-            pltpu.VMEM((n_mp, rank, slots), F32),
+            pltpu.VMEM((n_mp, 16, 128), BF16),
             pltpu.VMEM((n_dp, rank, units), F32),
-            pltpu.VMEM((n_mp, rank, slots), F32),
-            pltpu.VMEM((n_dp, rank, 256), F32),
+            pltpu.VMEM((n_mp, 16, 128), BF16),
+            pltpu.VMEM((n_dp, 1, piece), F32),
+            pltpu.VMEM((n_dp, 1, piece), F32),
+            pltpu.VMEM((n_mp, 1, piece + 128), F32),
             pltpu.VMEM((n_dp, rank, 256), F32),
             pltpu.VMEM((n_mp, rank, 256), F32),
-            pltpu.VMEM((n_dp, rank, 256), F32),
-            pltpu.VMEM((n_mp, rank, 256), F32),
-            pltpu.VMEM((n_dp, rank, 256), F32),
+            pltpu.VMEM((n_dp, 1, piece), F32),
             dma((9,)),
         ] + [dma(())] * 18 + [pltpu.SemaphoreType.REGULAR],
         compiler_params=pltpu.CompilerParams(

time: 62.3 us -> 60.5 us (0.971)
  Pallas kernels: 60.3 us -> 58.5 us
    pallas_call x1, Pallas kernels: 60.3 us -> 58.5 us  [shards(): pl.pallas_call(functools.partial(kernel, sizes, units * n_mp, slots // n_...]
where the time goes in v3:
time: 60.5 us; the launch traced here: 60.3 us
  Pallas kernels  58.5 us (97%)
  local copies, waits for them, and re-layouts  1.22 us (2%)
  between operations  0.64 us (1%)
    pallas_call x1, Pallas kernels, shards(): pl.pallas_call(functools.partial(kernel, sizes, units * n_mp, slots // n_...  58.5 us
    unnamed x2, local copies, waits for them, and re-layouts  1.22 us

profile of v3, /device:TPU:1, one launch (start us, length us, event | category | flops | bytes accessed | tf_op | source)
XLA Modules:
  0.0 60.3 jit_solution(15607084533677296487)
XLA Ops:
  0.6 58.5 %compress.1 = (f32[1,4,512]{2,1,0:T(4,128)S(1)}, f32[1,4,3072]{2,1,0:T(4,128)S(1)}) custom-call(bf16[192,128]{1,0:T(8,128)(2,1)} %bitcast.3, s32[2,128]{1,0:T(2,128)} %bitcast.4, f32[2,128]{1,0:T(2,128)} %bitcast.5, bf16[1,1,384,512]{3,2,1,0:T(8,128)(2,1)} %h_hbm.1, bf16[1,1,512,3072]{3,2,1,0:T(8,128)(2,1)} %e_hbm.1, f32[1,4,3072]{2,1,0:T(4,128)} %q_hbm.1), custom_call_target="tpu_custom_call" | custom-call | tf_op jit(solution)/shard_map/compress/pallas_call | solution.py:249
  59.1 0.6 copy.10
  59.7 0.6 %copy.11 = f32[1,4,3072]{2,1,0:T(4,128)} copy(f32[1,4,3072]{2,1,0:T(4,128)S(1)} %get-tuple-element.3) | data formatting | bytes 98304
